TPU v7x, 512 devices: a whole 4x4x16 slice. The times are simulated.
512 devices in a mesh: dp: 32 (over y, x, core), tensor: 16 (over z).
Axes of the slice: x: 4, y: 4, z: 16, core: 2. Of those that a mesh axis runs over, the one named last changes fastest.
Arguments:
- attention: bfloat16 [16384, 5120], P(('dp', 'tensor')), may hold values from -6 to 6
- residual: bfloat16 [16384, 5120], P('dp', 'tensor'), may hold values from -6 to 6
- output_weight: bfloat16 [5120, 5120], P(None, 'tensor'), may hold values from -0.078125 to 0.078125
- adapter_down_weight: bfloat16 [256, 5120, 64], P('dp', 'tensor'), may hold values from -0.078125 to 0.078125
- adapter_up_weight: bfloat16 [256, 64, 5120], P('dp', None, 'tensor'), may hold values from -0.75 to 0.75
- tenant: int32 [4096], P('dp'), may hold values from 0 to 255, as said below
- adapter_slot_index: int32 [256], replicated, may hold values from 0 to 255, as said below
Outputs:
- hidden: bfloat16 [16384, 5120], P('dp', 'tensor')
Inputs may be any that keep to these rules, and one draw needn't show every extreme that they name: With owner = adapter_slot_index[tenant] // 8: one index of dp, the same for all, is the owner of exactly 12 of the requests of every index of dp; every other index of dp owns at most 4 of the requests of one index of dp, and exactly 4 for some. A permutation: adapter a is row adapter_slot_index[a] of adapter_down_weight and adapter_up_weight.
All inputs are finite; a program needn't handle non-finite values.
Results may differ from a plain program's by a relative error of at most 0.0028.
Values may be sent and summed in bfloat16 or wider, within the bound.
A program may use at most 64 MiB of HBM per device.

v0:
```python
import jax
import jax.numpy as jnp
from jax import lax
from jax.sharding import PartitionSpec as P

adapter_scale = 0.5


def request_index(target_rows, chosen, slot_total):
    hits = (target_rows[None, :] == jnp.arange(slot_total, dtype=jnp.int32)[:, None]) & chosen[
        None, :
    ]
    numbers = jnp.arange(target_rows.shape[0], dtype=jnp.int32)[None, :] + 1
    return jnp.sum(jnp.where(hits, numbers, 0), axis=1) - 1


def shrink_term_rows(inputs, adapter_ids, adapter_a):
    adapter_total_count, slice_width, rank_size = adapter_a.shape
    stacked = adapter_a.transpose(1, 0, 2).reshape(slice_width, adapter_total_count * rank_size)
    all_terms = jnp.dot(inputs, stacked, preferred_element_type=jnp.float32).reshape(
        -1, adapter_total_count, rank_size
    )
    picked = adapter_ids[:, None] == jnp.arange(adapter_total_count, dtype=jnp.int32)[None, :]
    return jnp.sum(jnp.where(picked[:, :, None], all_terms, 0.0), axis=1)


def expand_term_rows(shrink_step, adapter_ids, adapter_b):
    adapter_total_count, rank_size, slice_width = adapter_b.shape
    picked = adapter_ids[:, None] == jnp.arange(adapter_total_count, dtype=jnp.int32)[None, :]
    spread = jnp.where(picked[:, :, None], shrink_step[:, None, :], jnp.zeros((), jnp.bfloat16))
    spread = spread.reshape(-1, adapter_total_count * rank_size)
    stacked = adapter_b.reshape(adapter_total_count * rank_size, slice_width)
    return jnp.dot(spread, stacked, preferred_element_type=jnp.float32).astype(jnp.bfloat16)


def local(
    attention,
    residual,
    output_weight,
    adapter_down_weight,
    adapter_up_weight,
    tenant,
    adapter_slot_index,
):
    data_parallel_size = lax.axis_size("dp")
    requests = tenant.shape[0]
    slice_width = output_weight.shape[1]
    token_count = residual.shape[0]
    draft_len = token_count // requests
    adapter_total_count = adapter_down_weight.shape[0]
    row_width_size = draft_len * slice_width
    column_start = lax.axis_index("tensor") * slice_width
    piece = lax.all_gather(attention, "tensor", axis=0, tiled=True)
    projected = jnp.dot(piece, output_weight, preferred_element_type=jnp.float32)
    own_columns = lax.dynamic_slice_in_dim(piece, column_start, slice_width, 1).astype(jnp.float32)
    combined = jnp.concatenate([projected, own_columns], axis=1)
    base_output = combined[:, :slice_width]
    own_slice = combined[:, slice_width:].astype(jnp.bfloat16)
    matches = tenant[:, None] == jnp.arange(adapter_slot_index.shape[0], dtype=jnp.int32)[None, :]
    request_slots = jnp.sum(jnp.where(matches, adapter_slot_index[None, :], 0), axis=1)
    owners = request_slots // adapter_total_count
    local_ids = request_slots % adapter_total_count
    owner_hits = (
        owners[:, None] == jnp.arange(data_parallel_size, dtype=jnp.int32)[None, :]
    ).astype(jnp.int32)
    positions = jnp.sum((jnp.cumsum(owner_hits, axis=0) - owner_hits) * owner_hits, axis=1)
    request_rows = own_slice.reshape(requests, row_width_size)
    slot_capacity = max(2, 3 * requests // data_parallel_size)
    target_rows = owners * slot_capacity + positions
    slot_table = request_index(
        target_rows, jnp.ones((requests,), bool), data_parallel_size * slot_capacity
    )
    filled = slot_table >= 0
    clipped = jnp.maximum(slot_table, 0)
    packed = jnp.where(filled[:, None], request_rows[clipped], jnp.zeros((), jnp.bfloat16))
    packed_ids = jnp.where(filled, local_ids[clipped], -1)
    got_rows, got_ids = (
        lax.all_to_all(
            packed.reshape(data_parallel_size, slot_capacity, row_width_size),
            "dp",
            split_axis=0,
            concat_axis=0,
            tiled=True,
        ),
        lax.all_to_all(
            packed_ids.reshape(data_parallel_size, slot_capacity),
            "dp",
            split_axis=0,
            concat_axis=0,
            tiled=True,
        ),
    )
    token_row_block = got_rows.reshape(-1, slice_width)
    token_index_list = jnp.repeat(got_ids.reshape(-1), draft_len)
    partial_value_sum = shrink_term_rows(token_row_block, token_index_list, adapter_down_weight)
    shrink_step = lax.psum(partial_value_sum, "tensor").astype(jnp.bfloat16)
    expanded_rows = expand_term_rows(shrink_step, token_index_list, adapter_up_weight)
    returned_rows = lax.all_to_all(
        expanded_rows.reshape(data_parallel_size, slot_capacity, row_width_size),
        "dp",
        split_axis=0,
        concat_axis=0,
        tiled=True,
    )
    adapter_rows = returned_rows.reshape(data_parallel_size * slot_capacity, row_width_size)[
        target_rows
    ]
    adapter_tokens = adapter_rows.reshape(residual.shape)
    total_output = (
        residual.astype(jnp.float32)
        + base_output
        + adapter_scale * adapter_tokens.astype(jnp.float32)
    )
    return total_output.astype(jnp.bfloat16)


def solution(mesh):
    in_specs = (
        P(("dp", "tensor"), None),
        P("dp", "tensor"),
        P(None, "tensor"),
        P("dp", "tensor", None),
        P("dp", None, "tensor"),
        P("dp"),
        P(),
    )
    out_specs = P("dp", "tensor")
    return jax.shard_map(local, mesh=mesh, in_specs=in_specs, out_specs=out_specs, check_vma=False)
```

profile of v0, /device:TPU:1, one launch (start us, length us, event | category | flops | bytes accessed | tf_op | source)
XLA Modules:
  0.0 260.4 jit_solution(9119175837200389018)
XLA Ops:
  6.5 0.7 all-gather.2.cloned.1.call-update
  7.3 1.1 select_reduce_fusion.1
  8.5 0.2 reduce_window_sum.11
  8.7 0.2 select_reduce_fusion.2
  8.8 0.1 select_reduce_fusion
  9.0 2.7 %gather_fusion = s32[384]{0:T(512)S(1)} fusion(s32[128]{0:T(128)S(1)} %get-tuple-element.8, s32[1024]{0:T(1024)S(1)} %pad_clamp_fusion.1), kind=kCustom, calls=%fused_computation | custom fusion | bytes 4608 | tf_op jit(solution)/shard_map/gather | solution.py:76
  11.7 0.7 select_n.84
  12.4 10.3 %all-to-all-start = ((s32[32,1,12]{2,1,0:T(1,128)}), s32[32,1,12]{2,1,0:T(1,128)S(1)}, u32[]{:S(2)}, u32[]{:S(2)}) async-start(s32[32,1,12]{2,1,0:T(1,128)} %bitcast), calls=%async_computation | async-start | bytes 32768 | tf_op jit(solution)/shard_map/all_to_all | solution.py:85
  22.9 66.5 %all-gather.2.cloned.1.call-done = bf16[512,5120]{1,0:T(8,128)(2,1)} async-done(((bf16[32,5120]{1,0:T(8,128)(2,1)}), bf16[512,5120]{1,0:T(8,128)(2,1)}) %all-gather.2.cloned.1.call-update) | async-done | bytes 5242896 | tf_op jit(solution)/shard_map/all_gather | solution.py:53
  89.4 2.0 constant_dynamic-slice_fusion
  91.4 2.1 reshape.214
  93.5 4.8 %gather_fusion.1 = bf16[384,1280]{1,0:T(8,128)(2,1)} fusion(bf16[128,1280]{1,0:T(8,128)(2,1)} %reshape.214, s32[1024]{0:T(1024)S(1)} %pad_clamp_fusion.1), kind=kCustom, calls=%fused_computation.1 | custom fusion | bytes 1967616 | tf_op jit(solution)/shard_map/gather | solution.py:75
  98.3 2.2 gather.13
  100.5 2.5 broadcast_select_fusion
  103.0 14.0 %all-to-all-start.1 = ((bf16[32,12,1280]{2,1,0:T(8,128)(2,1)}), bf16[32,12,1280]{2,1,0:T(8,128)(2,1)}, u32[]{:S(2)}, u32[]{:S(2)}) async-start(bf16[32,12,1280]{2,1,0:T(8,128)(2,1)} %broadcast_select_fusion), calls=%async_computation.1 | async-start | bytes 2621440 | tf_op jit(solution)/shard_map/all_to_all | solution.py:78
  117.1 0.5 broadcast.266
  117.6 0.7 reduce.3
  118.7 17.6 %all-to-all-done.1 = bf16[32,12,1280]{2,1,0:T(8,128)(2,1)} async-done(((bf16[32,12,1280]{2,1,0:T(8,128)(2,1)}), bf16[32,12,1280]{2,1,0:T(8,128)(2,1)}, u32[]{:S(2)}, u32[]{:S(2)}) %all-to-all-start.1) | async-done | bytes 983072 | tf_op jit(solution)/shard_map/all_to_all | solution.py:78
  136.2 3.6 %reshape.215 = bf16[1536,320]{1,0:T(8,128)(2,1)} reshape(bf16[32,12,1280]{2,1,0:T(8,128)(2,1)} %all-to-all-done.1) | data formatting | bytes 1966080 | tf_op jit(solution)/shard_map/reshape | solution.py:93
  139.9 3.1 %fusion.3 = f32[1536,64]{0,1:T(8,128)} fusion(pred[1536,8]{0,1:T(8,128)(4,1)S(1)} %iota_compare_fusion.3, bf16[1536,320]{1,0:T(8,128)(2,1)} %reshape.215, bf16[8,320,64]{1,2,0:T(8,128)(2,1)} %param.10), kind=kOutput, calls=%fused_computation.8 | convolution fusion | flops 504791040 | bytes 1716224 | tf_op jit(solution)/shard_map/dot_general | solution.py:20
  143.0 46.2 %all-reduce.1 = bf16[1536,64]{0,1:T(8,128)(2,1)S(1)} all-reduce(f32[1536,64]{0,1:T(8,128)} %fusion.3), channel_id=1, replica_groups=mesh['dp'=32,'tensor'=16] {'tensor'}, use_global_device_ids=true, to_apply=%region_5.6 | all-reduce | flops 98304 | bytes 589824 | tf_op jit(solution)/shard_map/psum | solution.py:96
  189.2 2.7 %fusion = bf16[1536,320]{0,1:T(8,128)(2,1)} fusion(bf16[8,64,320]{2,1,0:T(8,128)(2,1)} %param.11, pred[1536,8]{0,1:T(8,128)(4,1)S(1)} %iota_compare_fusion.3, bf16[1536,64]{0,1:T(8,128)(2,1)S(1)} %all-reduce.1), kind=kOutput, calls=%fused_computation.5 | convolution fusion | flops 504594432 | bytes 1519616 | tf_op jit(solution)/shard_map/dot_general | solution.py:33
  191.9 2.3 copy.16
  194.3 3.5 %reshape.217 = bf16[32,12,1280]{2,1,0:T(8,128)(2,1)} reshape(bf16[1536,320]{1,0:T(8,128)(2,1)} %copy.16) | data formatting | bytes 1966080 | tf_op jit(solution)/shard_map/reshape | solution.py:99
  197.8 19.3 %all-to-all-start.2 = ((bf16[32,12,1280]{2,1,0:T(8,128)(2,1)}), bf16[32,12,1280]{2,1,0:T(8,128)(2,1)}, u32[]{:S(2)}, u32[]{:S(2)}) async-start(bf16[32,12,1280]{2,1,0:T(8,128)(2,1)} %reshape.217), calls=%async_computation.2 | async-start | bytes 2621440 | tf_op jit(solution)/shard_map/all_to_all | solution.py:98
  217.2 19.2 %all-to-all-done.2 = bf16[32,12,1280]{2,1,0:T(8,128)(2,1)} async-done(((bf16[32,12,1280]{2,1,0:T(8,128)(2,1)}), bf16[32,12,1280]{2,1,0:T(8,128)(2,1)}, u32[]{:S(2)}, u32[]{:S(2)}) %all-to-all-start.2) | async-done | bytes 983072 | tf_op jit(solution)/shard_map/all_to_all | solution.py:98
  236.4 2.2 reshape.218
  238.5 3.2 %gather_fusion.2 = bf16[128,1280]{1,0:T(8,128)(2,1)} fusion(bf16[384,1280]{1,0:T(8,128)(2,1)} %reshape.218, s32[1024]{0:T(1024)S(1)} %pad_clamp_fusion), kind=kCustom, calls=%fused_computation.2 | custom fusion | bytes 655872 | tf_op jit(solution)/shard_map/gather | solution.py:105
  241.7 1.9 convert_multiply_fusion
  243.6 2.4 mul.44
  246.0 2.2 copy.17
  248.2 5.3 %fusion.5 = bf16[512,320]{0,1:T(8,128)(2,1)} fusion(f32[512,320]{0,1:T(8,128)} %copy.17, bf16[512,5120]{1,0:T(8,128)(2,1)} %all-gather.2.cloned.1.call-done, bf16[5120,320]{0,1:T(8,128)(2,1)S(1)} %copy-done, bf16[512,320]{0,1:T(8,128)(2,1)} %param.8), kind=kOutput, calls=%fused_computation.12 | convolution fusion | flops 1678376960 | bytes 9830400 | tf_op jit(solution)/shard_map/dot_general | solution.py:54
  (17 shorter events, 0.6 us)
Async XLA Ops:
  6.5 241.7 %copy-start = (bf16[5120,320]{0,1:T(8,128)(2,1)S(1)}, bf16[5120,320]{0,1:T(8,128)(2,1)}, u32[]{:S(2)}) copy-start(bf16[5120,320]{0,1:T(8,128)(2,1)} %param.9) | copy-start | bytes 9830404
  6.5 82.9 %all-gather.2.cloned.1.call-start = ((), (), s32[]{:S(2)}) async-start(), calls=%async_computation.3 | async-start | bytes 5570560 | tf_op jit(solution)/shard_map/all_gather | solution.py:53
  12.4 90.6 %all-to-all-start = ((s32[32,1,12]{2,1,0:T(1,128)}), s32[32,1,12]{2,1,0:T(1,128)S(1)}, u32[]{:S(2)}, u32[]{:S(2)}) async-start(s32[32,1,12]{2,1,0:T(1,128)} %bitcast), calls=%async_computation | async-start | bytes 32768 | tf_op jit(solution)/shard_map/all_to_all | solution.py:85
  103.0 33.2 %all-to-all-start.1 = ((bf16[32,12,1280]{2,1,0:T(8,128)(2,1)}), bf16[32,12,1280]{2,1,0:T(8,128)(2,1)}, u32[]{:S(2)}, u32[]{:S(2)}) async-start(bf16[32,12,1280]{2,1,0:T(8,128)(2,1)} %broadcast_select_fusion), calls=%async_computation.1 | async-start | bytes 2621440 | tf_op jit(solution)/shard_map/all_to_all | solution.py:78
  197.8 38.6 %all-to-all-start.2 = ((bf16[32,12,1280]{2,1,0:T(8,128)(2,1)}), bf16[32,12,1280]{2,1,0:T(8,128)(2,1)}, u32[]{:S(2)}, u32[]{:S(2)}) async-start(bf16[32,12,1280]{2,1,0:T(8,128)(2,1)} %reshape.217), calls=%async_computation.2 | async-start | bytes 2621440 | tf_op jit(solution)/shard_map/all_to_all | solution.py:98
Sparse Core Ops, SparseCore 0:
  9.4 79.9 all-gather.1
where the time goes:
time: 261 us; the launch traced here: 260 us
  waiting for transfers between devices  104 us (40%)
  blocking collectives  46.2 us (18%)
  starting transfers between devices  43.7 us (17%)
  local copies, waits for them, and re-layouts  34.9 us (13%)
  between operations  13.5 us (5%)
  matrix products  11.2 us (4%)
  other arithmetic  6.85 us (3%)
    all_gather x1, waiting for transfers between devices, local(): piece = lax.all_gather(attention, 'tensor', axis=0, tiled=True)  66.5 us
    psum x1, blocking collectives, local(): shrink_step = lax.psum(partial_value_sum, 'tensor').astype(jnp.bfloat16)  46.2 us
    all_to_all x1, starting transfers between devices, local(): lax.all_to_all(expanded_rows.reshape(data_parallel_size, slot_capacity, r...  19.3 us
    all_to_all x1, waiting for transfers between devices, local(): lax.all_to_all(expanded_rows.reshape(data_parallel_size, slot_capacity, r...  19.2 us
    all_to_all x1, waiting for transfers between devices, local(): lax.all_to_all(packed.reshape(data_parallel_size, slot_capacity, row_widt...  17.6 us
    all_to_all x1, starting transfers between devices, local(): lax.all_to_all(packed.reshape(data_parallel_size, slot_capacity, row_widt...  14 us
    all_to_all x1, starting transfers between devices, local(): lax.all_to_all(packed_ids.reshape(data_parallel_size, slot_capacity), 'dp...  10.3 us
    gather x2, local copies, waits for them, and re-layouts, local(): request_rows[clipped]  7.02 us
  transfers between devices with their start and end apart: 4, of which 3 were waited for; matrix products, arithmetic and copies ran while one was open for 8% of the time, Pallas kernels for 0%

commit v1 on v0

v1 whole, which is shorter than its diff:
```python
import jax
import jax.numpy as jnp
from jax import lax
from jax.experimental import pallas as pl
from jax.experimental.pallas import tpu as pltpu
from jax.sharding import PartitionSpec as P

BF = jnp.bfloat16
F32 = jnp.float32
ND, NZ = 32, 16
DRAFT, REQ, TOK = 4, 128, 512
WIDTH, COLS, RANK, ADP = 5120, 320, 64, 8
OWN = TOK // NZ
SLOT = TOK // ND
AROWS = 1536
ACH = AROWS // ND
BCH = ADP * RANK // ND
KCH = 512


def iota(shape, axis):
    return lax.broadcasted_iota(jnp.int32, shape, axis)


def dot(a, b):
    return jnp.dot(a, b, preferred_element_type=F32)


def dot_t(a, b):
    return lax.dot_general(a, b, (((0,), (0,)), ((), ())), preferred_element_type=F32)


def onehot(mask):
    return jnp.where(mask, 1.0, 0.0).astype(BF)


def routing(tenant, index, me):
    hit = onehot(iota((2 * REQ, REQ), 0) == tenant)
    slot = dot(jnp.broadcast_to(index, (8, 2 * REQ)).astype(F32).astype(BF), hit)[0:1]
    owner = jnp.floor(slot * (1.0 / ADP))
    adapter = slot - ADP * owner
    owner_id = iota((ND, REQ), 0).astype(F32)
    own_hit = jnp.where(owner_id == owner, 1.0, 0.0)
    before = onehot(iota((REQ, REQ), 0) < iota((REQ, REQ), 1))
    place = jnp.sum(own_hit * dot(own_hit.astype(BF), before), axis=0, keepdims=True)
    count = jnp.sum(own_hit, axis=1, keepdims=True)
    busy = jnp.where(count > 4.5, 1.0, 0.0)
    busy_req = jnp.sum(own_hit * busy, axis=0, keepdims=True)
    count = jnp.broadcast_to(count * (1.0 - busy), (ND, REQ)).astype(BF)
    is_busy = jnp.sum(busy * jnp.where(owner_id[:, 0:1] == me.astype(F32), 1.0, 0.0), axis=0, keepdims=True)
    slot_row = iota((REQ, REQ), 0)
    filled = dot(onehot(iota((REQ, ND), 0) // 4 == iota((REQ, ND), 1)), count)
    free = jnp.where((slot_row % 4).astype(F32) >= filled, 1.0, 0.0)
    rank = dot(onehot(iota((REQ, REQ), 1) < slot_row), free.astype(BF))
    to_free = free * jnp.where(rank == place, 1.0, 0.0) * busy_req
    to_own = jnp.where(slot_row.astype(F32) == 4.0 * owner + place, 1.0, 0.0) * (1.0 - busy_req)
    by_request = (to_free + to_own).astype(BF)
    spread = onehot(iota((REQ, TOK), 0) == iota((REQ, TOK), 1) // DRAFT)
    gather = onehot(iota((TOK, REQ), 0) // DRAFT == iota((TOK, REQ), 1))
    rows = dot(dot(gather, by_request).astype(BF), spread)
    same = iota((TOK, TOK), 0) % DRAFT == iota((TOK, TOK), 1) % DRAFT
    matrix = jnp.where(same, rows, 0.0).astype(BF)
    ident = adapter + 1.0 + ADP * busy_req
    eye = iota((REQ, REQ), 0) == iota((REQ, REQ), 1)
    column = jnp.sum(jnp.where(eye, ident, 0.0), axis=1, keepdims=True)
    ids = dot(gather, jnp.broadcast_to(column, (REQ, 64)).astype(BF)).astype(BF)
    return matrix, ids, is_busy


def kernel(att, res_h, w_h, a_h, b_h, ten, idx, out, w, res, av, bv, apk, asnd, bsnd, arcv, brcv, ahot, bhot,
           snd, own, pick, pk, prcv, zs, zr, red, sh, er, back, buf, base,
           lsem, sa, ra, sg, rg, shs, shr, sha, sra, sd, rd, sz, rz, sy, ry, sb, rb):
    d = lax.axis_index("dp")
    z = lax.axis_index("tensor")

    def copy(src, dst, ss, rs, dev):
        return pltpu.make_async_remote_copy(src_ref=src, dst_ref=dst, send_sem=ss, recv_sem=rs, device_id=dev,
                                            device_id_type=pl.DeviceIdType.MESH)

    def zdev(i):
        return (d, lax.rem(z + i, NZ))

    def ddev(i):
        return (lax.rem(d + i, ND), z)

    def each(n, f):
        def body(i, carry):
            f(i)
            return carry
        lax.fori_loop(1, n, body, 0)

    barrier = pltpu.get_barrier_semaphore()
    each(NZ, lambda i: pl.semaphore_signal(barrier, inc=1, device_id=zdev(i), device_id_type=pl.DeviceIdType.MESH))
    each(ND, lambda i: pl.semaphore_signal(barrier, inc=1, device_id=ddev(i), device_id_type=pl.DeviceIdType.MESH))
    loads = [pltpu.make_async_copy(h, v, lsem.at[i]) for i, (h, v) in
             enumerate(((a_h, av), (b_h, bv), (w_h, w), (res_h, res)))]
    for load in loads:
        load.start()
    for t in range(NZ):
        snd[t] = att[:, COLS * t:COLS * t + COLS]
    matrix, ids, is_busy = routing(ten[...], idx[...], d)
    pick[...] = matrix
    own[z] = snd[z]
    loads[0].wait()
    loads[1].wait()
    mine = is_busy.astype(BF)
    for e in range(4):
        pair = jnp.concatenate([av[e], av[e + 4]], axis=1)
        apk[COLS * e:COLS * e + COLS] = pair
        asnd[COLS * e:COLS * e + COLS] = pair * mine
    asnd[4 * COLS:] = jnp.zeros((AROWS - 4 * COLS, 128), BF)
    for e in range(ADP):
        bsnd[RANK * e:RANK * e + RANK] = bv[e] * mine
    arcv[d] = asnd[pl.ds(pl.multiple_of(d * ACH, 16), ACH)]
    brcv[d] = bsnd[pl.ds(pl.multiple_of(d * BCH, 16), BCH)]
    pl.semaphore_wait(barrier, NZ + ND - 2)

    def slices(i):
        to = lax.rem(z + i, NZ)
        return copy(snd.at[to], own.at[z], sa.at[i], ra.at[i], (d, to))

    each(NZ, lambda i: slices(i).start())

    right, left = zdev(1), zdev(NZ - 1)

    def ring(way, step, half):
        block = lax.rem(z + (NZ - step if way == 0 else step), NZ)
        dst = buf.at[block, pl.ds(16 * half, 16)]
        src = att.at[pl.ds(16 * half, 16)] if step == 0 else dst
        return copy(src, dst, sg.at[way, step, half], rg.at[way, step, half], right if way == 0 else left)

    def moves(step):
        return [(way, half) for half in range(2) for way in range(2) if step < 7 or way == half]

    def ring_step(step):
        for way, half in moves(step):
            if step > 0:
                ring(way, step - 1, half).wait_recv()
            ring(way, step, half).start()

    ring_step(0)

    def scatter(i):
        to = lax.rem(d + i, ND)
        return (copy(asnd.at[pl.ds(pl.multiple_of(to * ACH, 16), ACH)], arcv.at[d], shs.at[i], shr.at[i], (to, z)),
                copy(bsnd.at[pl.ds(pl.multiple_of(to * BCH, 16), BCH)], brcv.at[d], sha.at[i], sra.at[i], (to, z)))

    def spread_hot(i):
        return (copy(ahot.at[d], ahot.at[d], shs.at[ND + i], shr.at[ND + i], ddev(i)),
                copy(bhot.at[d], bhot.at[d], sha.at[ND + i], sra.at[ND + i], ddev(i)))

    def start_both(pair):
        pair[0].start()
        pair[1].start()

    def wait_both(pair):
        pair[0].wait_recv()
        pair[1].wait_recv()

    def sent_both(pair):
        pair[0].wait_send()
        pair[1].wait_send()

    each(ND, lambda i: start_both(scatter(i)))
    buf[z] = att[...]
    each(ND, lambda i: wait_both(scatter(i)))
    ahot[d] = jnp.sum(arcv[...].astype(F32), axis=0).astype(BF)
    bhot[d] = jnp.sum(brcv[...].astype(F32), axis=0).astype(BF)
    each(ND, lambda i: start_both(spread_hot(i)))

    each(NZ, lambda i: slices(i).wait_recv())
    ext = jnp.concatenate([own[...].reshape(TOK, COLS), ids], axis=1)
    pk[...] = dot(pick[...], ext).astype(BF).reshape(ND, SLOT, COLS + 64)
    prcv[d] = pk[d]

    def deliver(i):
        to = lax.rem(d + i, ND)
        return copy(pk.at[to], prcv.at[d], sd.at[i], rd.at[i], (to, z))

    each(ND, lambda i: deliver(i).start())
    ring_step(1)
    each(ND, lambda i: wait_both(spread_hot(i)))
    each(ND, lambda i: deliver(i).wait_recv())
    got = prcv[...].reshape(TOK, COLS + 64)
    rows, ident = got[:, :COLS], got[:, COLS:COLS + 1].astype(F32)
    upper = jnp.where(iota((1, 128), 1) < RANK, 0.0, 4.0)
    hot_a = ahot[...].reshape(AROWS, 128)
    total = jnp.zeros((TOK, 128), F32)
    for e in range(4):
        lane_id = upper + (e + 1.0)
        total += jnp.where(ident == lane_id, dot(rows, apk[COLS * e:COLS * e + COLS]), 0.0)
        total += jnp.where(ident == lane_id + ADP, dot(rows, hot_a[COLS * e:COLS * e + COLS]), 0.0)
    part = (total[:, :RANK] + total[:, RANK:]).astype(BF)
    for t in range(NZ):
        zs[t] = jnp.concatenate([part[32 * t:32 * t + 16], part[32 * t + 16:32 * t + 32]], axis=1)
    zr[z] = zs[z]

    def reduce(i):
        to = lax.rem(z + i, NZ)
        return copy(zs.at[to], zr.at[z], sz.at[i], rz.at[i], (d, to))

    def share(i):
        return copy(red.at[z], red.at[z], sy.at[i], ry.at[i], zdev(i))

    each(NZ, lambda i: reduce(i).start())
    ring_step(2)
    each(NZ, lambda i: reduce(i).wait_recv())
    red[z] = jnp.sum(zr[...].astype(F32), axis=0).astype(BF)
    each(NZ, lambda i: share(i).start())
    ring_step(3)
    each(NZ, lambda i: share(i).wait_recv())
    for t in range(NZ):
        sh[32 * t:32 * t + 16] = red[t, :, :RANK]
        sh[32 * t + 16:32 * t + 32] = red[t, :, RANK:]
    wide = jnp.concatenate([sh[...]] * ADP, axis=1)
    group = (iota((1, ADP * RANK), 1) // RANK + 1).astype(F32)
    zero = jnp.zeros((), BF)
    expand = dot(jnp.where(ident == group, wide, zero), bv[...].reshape(ADP * RANK, COLS))
    expand += dot(jnp.where(ident == group + ADP, wide, zero), bhot[...].reshape(ADP * RANK, COLS))
    er[...] = expand.astype(BF).reshape(ND, SLOT, COLS)
    back[d] = er[d]

    def give_back(i):
        to = lax.rem(d + i, ND)
        return copy(er.at[to], back.at[d], sb.at[i], rb.at[i], (to, z))

    each(ND, lambda i: give_back(i).start())
    ring_step(4)
    loads[2].wait()
    loads[3].wait()

    def project(steps):
        blocks = [lax.rem(z + s + NZ, NZ) for s in steps]

        def body(k, acc):
            at = pl.ds(pl.multiple_of(k * KCH, KCH), KCH)
            x = jnp.concatenate([buf[b, :, at] for b in blocks], axis=0)
            return acc + dot(x, w[at, :])

        acc = lax.fori_loop(0, WIDTH // KCH, body, jnp.zeros((OWN * len(blocks), COLS), F32))
        for n, b in enumerate(blocks):
            base[pl.ds(pl.multiple_of(b * OWN, OWN), OWN)] = acc[OWN * n:OWN * n + OWN]

    project([0, -1, 1, -2, 2, -3, 3, -4, 4])
    ring_step(5)
    each(ND, lambda i: give_back(i).wait_recv())
    extra = dot_t(pick[...], back[...].reshape(TOK, COLS))
    ring_step(6)
    project([-5, 5, -6, 6])
    ring_step(7)
    for way, half in moves(6):
        if (way, half) not in moves(7):
            ring(way, 6, half).wait_recv()
    for way, half in moves(7):
        ring(way, 7, half).wait_recv()
    project([-7, 7, 8])
    out[...] = (res[...].astype(F32) + base[...] + 0.5 * extra).astype(BF)

    for step in range(8):
        for way, half in moves(step):
            ring(way, step, half).wait_send()
    each(NZ, lambda i: slices(i).wait_send())
    each(NZ, lambda i: reduce(i).wait_send())
    each(NZ, lambda i: share(i).wait_send())
    each(ND, lambda i: sent_both(scatter(i)))
    each(ND, lambda i: sent_both(spread_hot(i)))
    each(ND, lambda i: deliver(i).wait_send())
    each(ND, lambda i: give_back(i).wait_send())


def local(attention, residual, output_weight, adapter_down_weight, adapter_up_weight, tenant, adapter_slot_index):
    vmem = pl.BlockSpec(memory_space=pltpu.VMEM)
    hbm = pl.BlockSpec(memory_space=pl.ANY)
    dma = pltpu.SemaphoreType.DMA

    def held(*shape, dtype=BF):
        return pltpu.VMEM(shape, dtype)

    return pl.pallas_call(
        kernel,
        out_shape=jax.ShapeDtypeStruct((TOK, COLS), BF),
        in_specs=[vmem, hbm, hbm, hbm, hbm, vmem, vmem],
        out_specs=vmem,
        scratch_shapes=[
            held(WIDTH, COLS), held(TOK, COLS), held(ADP, COLS, RANK), held(ADP, RANK, COLS),
            held(4 * COLS, 128), held(AROWS, 128), held(ADP * RANK, COLS),
            held(ND, ACH, 128), held(ND, BCH, COLS), held(ND, ACH, 128), held(ND, BCH, COLS),
            held(NZ, OWN, COLS), held(NZ, OWN, COLS), held(TOK, TOK),
            held(ND, SLOT, COLS + 64), held(ND, SLOT, COLS + 64),
            held(NZ, 16, 128), held(NZ, 16, 128), held(NZ, 16, 128), held(TOK, RANK),
            held(ND, SLOT, COLS), held(ND, SLOT, COLS),
            held(NZ, OWN, WIDTH), held(TOK, COLS, dtype=F32),
            dma((4,)), dma((NZ,)), dma((NZ,)), dma((2, 8, 2)), dma((2, 8, 2)),
            dma((2 * ND,)), dma((2 * ND,)), dma((2 * ND,)), dma((2 * ND,)),
            dma((ND,)), dma((ND,)), dma((NZ,)), dma((NZ,)), dma((NZ,)), dma((NZ,)), dma((ND,)), dma((ND,)),
        ],
        compiler_params=pltpu.CompilerParams(collective_id=0, has_side_effects=True, vmem_limit_bytes=56 * 2**20),
    )(attention, residual, output_weight, adapter_down_weight, adapter_up_weight,
      tenant.reshape(1, REQ), adapter_slot_index.reshape(1, 2 * REQ))


def solution(mesh):
    in_specs = (
        P(("dp", "tensor"), None),
        P("dp", "tensor"),
        P(None, "tensor"),
        P("dp", "tensor", None),
        P("dp", None, "tensor"),
        P("dp"),
        P(),
    )
    return jax.shard_map(local, mesh=mesh, in_specs=in_specs, out_specs=P("dp", "tensor"), check_vma=False)
```

time: 261 us -> 115 us (0.44)
  waiting for transfers between devices: 104 us -> 0 us
  Pallas kernels: 0 us -> 103 us
  blocking collectives: 46.2 us -> 0 us
  starting transfers between devices: 43.7 us -> 0 us
  local copies, waits for them, and re-layouts: 34.9 us -> 11.7 us
  between operations: 13.5 us -> 0.01 us
  matrix products: 11.2 us -> 0 us
  other arithmetic: 6.85 us -> 0 us
    pallas_call x0 -> x1, Pallas kernels: none -> 103 us  [local(): pl.pallas_call(kernel, out_shape=jax.ShapeDtypeStruct((TOK, COLS), BF), i...]
    all_gather x1 -> x0, waiting for transfers between devices: 66.5 us -> none  [local(): piece = lax.all_gather(attention, 'tensor', axis=0, tiled=True)]
    psum x1 -> x0, blocking collectives: 46.2 us -> none  [local(): shrink_step = lax.psum(partial_value_sum, 'tensor').astype(jnp.bfloat16)]
    all_to_all x3 -> x0, starting transfers between devices: 43.7 us -> none  [the longest x1 19.3 us: local(): lax.all_to_all(expanded_rows.reshape(data_parallel_size, slot_capacity, r...]
    all_to_all x3 -> x0, waiting for transfers between devices: 36.7 us -> none  [the longest x1 19.2 us: local(): lax.all_to_all(expanded_rows.reshape(data_parallel_size, slot_capacity, r...]
    gather x4 -> x0, local copies, waits for them, and re-layouts: 12.9 us -> none  [the longest x2 7.02 us: local(): request_rows[clipped]]
    reshape x5 -> x0, local copies, waits for them, and re-layouts: 11.5 us -> none  [the longest x1 3.64 us: local(): token_row_block = got_rows.reshape(-1, slice_width)]
    dot_general x3 -> x0, matrix products: 11.2 us -> none  [the longest x1 5.32 us: local(): jnp.dot(piece, output_weight, preferred_element_type=jnp.float32)]
  transfers between devices with their start and end apart: 4 -> 0, of which waited for: 3 -> 0; matrix products, arithmetic and copies ran while one was open for 8% -> 0% of each run, Pallas kernels for 0% -> 0%
where the time goes in v1:
time: 115 us
  Pallas kernels  103 us (90%)
  local copies, waits for them, and re-layouts  11.7 us (10%)
    pallas_call x1, Pallas kernels, local(): pl.pallas_call(kernel, out_shape=jax.ShapeDtypeStruct((TOK, COLS), BF), i...  103 us
    unnamed x3, local copies, waits for them, and re-layouts  9.83 us

profile of v1, /device:TPU:1, one launch (start us, length us, event | category | flops | bytes accessed | tf_op | source)
XLA Modules:
  0.0 114.6 jit_solution(5454910070786102271)
XLA Ops:
  0.0 1.9 %copy.8.res_h = bf16[512,320]{1,0:T(8,128)(2,1)} copy(bf16[512,320]{0,1:T(8,128)(2,1)} %param.8) | data formatting | bytes 655360 | tf_op args[1]
  1.9 2.1 %copy.10.a_h = bf16[8,320,64]{2,1,0:T(8,128)(2,1)} copy(bf16[8,320,64]{1,2,0:T(8,128)(2,1)} %param.10) | data formatting | bytes 655360 | tf_op args[3]
  4.0 5.8 %copy.9.w_h = bf16[5120,320]{1,0:T(8,128)(2,1)} copy(bf16[5120,320]{0,1:T(8,128)(2,1)} %param.9) | data formatting | bytes 6553600 | tf_op args[2]
  9.8 102.9 %shard_map.73 = bf16[512,320]{1,0:T(8,128)(2,1)} custom-call(bf16[32,5120]{1,0:T(8,128)(2,1)} %att.1, bf16[512,320]{1,0:T(8,128)(2,1)} %copy.8.res_h, bf16[5120,320]{1,0:T(8,128)(2,1)} %copy.9.w_h, bf16[8,320,64]{2,1,0:T(8,128)(2,1)} %copy.10.a_h, bf16[8,64,320]{2,1,0:T(8,128)(2,1)} %b_h.1, s32[1,128]{1,0:T(1,128)} %bitcast.3, s32[1,256]{1,0:T(1,128)} %bitcast.2), custom_call_target="tpu_custom_call" | custom-call | tf_op jit(solution)/shard_map/pallas_call | solution.py:279
  112.7 1.9 %copy.11 = bf16[512,320]{0,1:T(8,128)(2,1)} copy(bf16[512,320]{1,0:T(8,128)(2,1)} %shard_map.73) | data formatting | bytes 655360 | tf_op jit(solution)/shard_map/pallas_call | solution.py:279

commit v2 on v1

v2 whole, which is shorter than its diff:
```python
import jax
import jax.numpy as jnp
from jax import lax
from jax.experimental import pallas as pl
from jax.experimental.pallas import tpu as pltpu
from jax.sharding import PartitionSpec as P

BF = jnp.bfloat16
F32 = jnp.float32
ND, NZ = 32, 16
DRAFT, REQ, TOK = 4, 128, 512
WIDTH, COLS, RANK, ADP = 5120, 320, 64, 8
OWN = TOK // NZ
SLOT = TOK // ND
HOT = ADP * RANK
HALF = WIDTH // 2
NC = 16
MAIN, REST = 256, 64
QUART = HALF // 4
LANES = HALF + QUART
CUT = 1664


def iota(shape, axis):
    return lax.broadcasted_iota(jnp.int32, shape, axis)


def dot(a, b):
    return jnp.dot(a, b, preferred_element_type=F32)


def dot_t(a, b):
    return lax.dot_general(a, b, (((0,), (0,)), ((), ())), preferred_element_type=F32)


def onehot(mask):
    return jnp.where(mask, 1.0, 0.0).astype(BF)


def dot_nt(a, b):
    return lax.dot_general(a, b, (((1,), (1,)), ((), ())), preferred_element_type=F32)


def routing(tenant, index, me):
    hit = onehot(iota((2 * REQ, REQ), 0) == tenant)
    slot = dot(jnp.broadcast_to(index, (8, 2 * REQ)).astype(F32).astype(BF), hit)[0:1]
    owner = jnp.floor(slot * (1.0 / ADP))
    adapter = slot - ADP * owner
    owner_id = iota((ND, REQ), 0).astype(F32)
    own_hit = jnp.where(owner_id == owner, 1.0, 0.0)
    before = onehot(iota((REQ, REQ), 0) < iota((REQ, REQ), 1))
    place = jnp.sum(own_hit * dot(own_hit.astype(BF), before), axis=0, keepdims=True)
    count = jnp.sum(own_hit, axis=1, keepdims=True)
    busy = jnp.where(count > 4.5, 1.0, 0.0)
    busy_req = jnp.sum(own_hit * busy, axis=0, keepdims=True)
    count = jnp.broadcast_to(count * (1.0 - busy), (ND, REQ)).astype(BF)
    is_busy = jnp.sum(busy * jnp.where(owner_id[:, 0:1] == me.astype(F32), 1.0, 0.0), axis=0, keepdims=True)
    slot_row = iota((REQ, REQ), 0)
    filled = dot(onehot(iota((REQ, ND), 0) // 4 == iota((REQ, ND), 1)), count)
    free = jnp.where((slot_row % 4).astype(F32) >= filled, 1.0, 0.0)
    rank = dot(onehot(iota((REQ, REQ), 1) < slot_row), free.astype(BF))
    to_free = free * jnp.where(rank == place, 1.0, 0.0) * busy_req
    to_own = jnp.where(slot_row.astype(F32) == 4.0 * owner + place, 1.0, 0.0) * (1.0 - busy_req)
    by_request = (to_free + to_own).astype(BF)
    spread = onehot(iota((REQ, TOK), 0) == iota((REQ, TOK), 1) // DRAFT)
    gather = onehot(iota((TOK, REQ), 0) // DRAFT == iota((TOK, REQ), 1))
    rows = dot(dot(gather, by_request).astype(BF), spread)
    same = iota((TOK, TOK), 0) % DRAFT == iota((TOK, TOK), 1) % DRAFT
    matrix = jnp.where(same, rows, 0.0).astype(BF)
    ident = adapter + 1.0 + ADP * busy_req
    eye = iota((REQ, REQ), 0) == iota((REQ, REQ), 1)
    column = jnp.sum(jnp.where(eye, ident, 0.0), axis=1, keepdims=True)
    ids = dot(gather, jnp.broadcast_to(column, (REQ, 64)).astype(BF)).astype(BF)
    return matrix, ids, is_busy


def kernel(att, res_h, w_h, a_h, b_h, ten, idx, out, wr, res, av, bv, mine, twin_in, half, hot_in, hot,
           snd, own, pick, pk, prcv, zs, zr, red, sh, er, back, buf, wg, rsnd, rrcv, psnd, pout,
           lsem, sems, sx, rx, sw, rw, ss, rs):
    d = lax.axis_index("dp")
    z = lax.axis_index("tensor")
    core = lax.rem(d, 2)
    chip = lax.div(d, 2)
    x, y = lax.rem(chip, 4), lax.div(chip, 4)

    def copy(src, dst, ss, rs, dev):
        return pltpu.make_async_remote_copy(src_ref=src, dst_ref=dst, send_sem=ss, recv_sem=rs, device_id=dev,
                                            device_id_type=pl.DeviceIdType.MESH)

    def each(n, f):
        def body(i, carry):
            f(i)
            return carry
        lax.fori_loop(1, n, body, 0)

    twin = (d + 1 - 2 * core, z)
    opened = []

    class Flow:
        def __init__(self, n, src, dst, to, number):
            self.n, self.src, self.dst, self.to = n, src, dst, to
            self.sems = (sems.at[0, number], sems.at[1, number])
            self.got = False

        def one(self, i):
            dev, source, place = self.to(i)
            copy(self.src.at[source], self.dst.at[place], *self.sems, dev).start()

        def start(self):
            each(self.n, self.one)
            opened.append(self)

        def all(self):
            ref = self.src.at[pl.ds(0, self.n - 1)]
            return copy(ref, ref, *self.sems, twin)

        def recv(self):
            self.all().wait_recv()
            self.got = True

        def sent(self):
            self.all().wait_send()
            opened.remove(self)

    class Single:
        def __init__(self, c):
            self.c, self.got = c, False

        def start(self):
            self.c.start()
            opened.append(self)

        def recv(self):
            self.c.wait_recv()
            self.got = True

        def sent(self):
            self.c.wait_send()
            opened.remove(self)

    def finish():
        for flow in list(opened):
            if not flow.got:
                flow.recv()
            flow.sent()

    def over_z(i):
        to = lax.rem(z + i, NZ)
        return (d, to), to, z

    def over_z_same(i):
        return (d, lax.rem(z + i, NZ)), z, z

    def over_dp(i):
        to = lax.rem(d + i, ND)
        return (to, z), to, d

    def over_chips(i):
        to = lax.rem(chip + i, NC)
        return (2 * to + core, z), to, chip

    def over_chips_same(i):
        return (2 * lax.rem(chip + i, NC) + core, z), chip, chip

    slices = Flow(NZ, snd, own, over_z, 0)
    deliver = Flow(ND, pk, prcv, over_dp, 1)
    reduce = Flow(NZ, zs, zr, over_z, 2)
    share = Flow(NZ, red, red, over_z_same, 3)
    give_back = Flow(ND, er, back, over_dp, 4)
    results = Flow(NZ, rsnd, rrcv, over_z, 5)
    plane = Flow(NC, psnd, pout, over_chips, 6)
    scatter = Flow(NC, half, hot_in, over_chips, 7)
    gather = Flow(NC, hot.at[core], hot.at[core], over_chips_same, 8)
    swap = Single(copy(mine.at[1 - core], twin_in, sems.at[0, 9], sems.at[1, 9], twin))
    swap_hot = Single(copy(hot.at[core], hot.at[core], sems.at[0, 10], sems.at[1, 10], twin))

    first = x * (1 - core) + y * core
    second = y * (1 - core) + x * core

    def spot(a, b):
        return lax.rem(a, 4) * (1 + 3 * core) + lax.rem(b, 4) * (4 - 3 * core)

    def pdev(a, b):
        return (2 * spot(a, b) + core, z)

    near1 = (pdev(first + 1, second), pdev(first + 3, second))
    near2 = (pdev(first, second + 1), pdev(first, second + 3))
    kept = {}

    def keep(key, make):
        if key not in kept:
            kept[key] = Single(make())
        return kept[key]

    def line(way, hop):
        def make():
            if hop == 0:
                return copy(att, buf.at[chip], sx.at[0, way, 0], rx.at[0, way, 0], near1[way])
            ref = buf.at[spot(first + (3 if way == 0 else 1), second), pl.ds(16 * way, 16)]
            return copy(ref, ref, sx.at[0, way, 1], rx.at[0, way, 1], near1[way])
        return keep(("line", way, hop), make)

    def sheet(way, hop, j):
        def make():
            col = first + (0, 3, 1, 2)[j]
            if hop == 0:
                dst = buf.at[spot(col, second)]
                src = att if j == 0 else dst
            else:
                dst = buf.at[spot(col, second + (3 if way == 0 else 1)), pl.ds(16 * way, 16)]
                src = dst
            return copy(src, dst, sx.at[1 + hop, way, j], rx.at[1 + hop, way, j], near2[way])
        return keep(("sheet", way, hop, j), make)

    right, left = (d, lax.rem(z + 1, NZ)), (d, lax.rem(z + NZ - 1, NZ))

    def ring(way, step, part):
        def make():
            block = lax.rem(z + (NZ - step if way == 0 else step), NZ)
            lanes = pl.ds(0, CUT) if part == 0 else pl.ds(CUT, LANES - CUT)
            ref = wg.at[core, block, :, lanes]
            return copy(ref, ref, sw.at[way, step, part], rw.at[way, step, part], right if way == 0 else left)
        return keep(("ring", way, step, part), make)

    def moves(step):
        return [(way, part) for part in range(2) for way in range(2) if step < 7 or way == part]

    def tell(o):
        def make():
            ref = wg.at[core, lax.rem(z + o, NZ)]
            return copy(ref, ref, ss.at[o], rs.at[o], twin)
        return keep(("tell", o), make)

    def ring_step(step):
        for way, part in moves(step):
            if step > 0:
                ring(way, step - 1, part).recv()
            ring(way, step, part).start()
        if step == 0:
            tell(0).start()
        elif step < 7:
            tell(step).start()
            tell(NZ - step).start()

    def ring_end():
        for way, part in moves(6):
            if not ring(way, 6, part).got:
                ring(way, 6, part).recv()
        tell(7).start()
        tell(9).start()
        for way, part in moves(7):
            ring(way, 7, part).recv()
        tell(8).start()

    def line_on():
        for way in range(2):
            line(way, 0).recv()
            line(way, 1).start()
            for to in range(2):
                sheet(to, 0, 1 + way).start()

    def line_end():
        for way in range(2):
            line(way, 1).recv()
        for to in range(2):
            sheet(to, 0, 3).start()

    def sheet_on(j):
        for way in range(2):
            sheet(way, 0, j).recv()
            sheet(way, 1, j).start()

    barrier = pltpu.get_barrier_semaphore()
    each(NZ, lambda i: pl.semaphore_signal(barrier, inc=1, device_id=over_z(i)[0], device_id_type=pl.DeviceIdType.MESH))
    each(ND, lambda i: pl.semaphore_signal(barrier, inc=1, device_id=over_dp(i)[0], device_id_type=pl.DeviceIdType.MESH))
    lanes_half = pl.ds(pl.multiple_of(core * HALF, HALF), HALF)
    loads = [pltpu.make_async_copy(h, v, lsem.at[i]) for i, (h, v) in enumerate((
        (w_h.at[pl.ds(pl.multiple_of(16 * chip, 16), 16), lanes_half], wg.at[core, z, :, pl.ds(0, HALF)]),
        (w_h.at[pl.ds(MAIN, REST), lanes_half], wr), (a_h, av), (b_h, bv), (res_h, res)))]
    for load in loads:
        load.start()
    for t in range(NZ):
        snd[t] = att[:, COLS * t:COLS * t + COLS]
    own[z] = snd[z]
    matrix, ids, is_busy = routing(ten[...], idx[...], d)
    pick[...] = matrix
    for load in loads:
        load.wait()
    n, c = iota((16, REST), 0), iota((16, REST), 1)
    low = dot(onehot((c == 4 * chip + n) & (n < 4)), wr[...])
    wg[core, z, :, HALF:] = jnp.concatenate([low[:4, QUART * q:QUART * q + QUART] for q in range(4)], axis=0).astype(BF)
    mark = is_busy.astype(BF)
    for i in range(2 * NC):
        e, r = i // 4, 16 * (i % 4)
        mine[i // NC, i % NC, :16] = av[e, r:r + 16] * mark
        mine[i // NC, i % NC, 16:] = bv[e, r:r + 16] * mark
    pl.semaphore_wait(barrier, NZ + ND - 2)

    slices.start()
    for way in range(2):
        line(way, 0).start()
    for way in range(2):
        sheet(way, 0, 0).start()
    swap.start()
    buf[chip] = att[...]
    swap.recv()
    half[...] = mine[core] + twin_in[...]
    hot_in[chip] = half[chip]
    scatter.start()
    line_on()
    sheet_on(0)
    line_end()
    scatter.recv()
    hot[core, chip] = jnp.sum(hot_in[...].astype(F32), axis=0).astype(BF)
    gather.start()
    ring_step(0)
    sheet_on(1)
    ring_step(1)
    sheet_on(2)
    ring_step(2)
    slices.recv()
    ext = jnp.concatenate([own[...].reshape(TOK, COLS), ids], axis=1)
    pk[...] = dot(pick[...], ext).astype(BF).reshape(ND, SLOT, COLS + 64)
    prcv[d] = pk[d]
    deliver.start()
    ring_step(3)
    sheet_on(3)
    ring_step(4)
    gather.recv()
    swap_hot.start()
    deliver.recv()
    swap_hot.recv()
    got = prcv[...].reshape(TOK, COLS + 64)
    rows, ident = got[:, :COLS], got[:, COLS:COLS + 1].astype(F32)
    group = (iota((1, HOT), 1) // RANK + 1).astype(F32)
    hot_all = hot[...].reshape(ND, 32, COLS)
    hot_a, hot_b = hot_all[:, :16].reshape(HOT, COLS), hot_all[:, 16:].reshape(HOT, COLS)
    total = jnp.where(ident == group, dot_nt(rows, av[...].reshape(HOT, COLS)), 0.0)
    total += jnp.where(ident == group + ADP, dot_nt(rows, hot_a), 0.0)
    total = total[:, :128] + total[:, 128:256] + total[:, 256:384] + total[:, 384:]
    part = (total[:, :RANK] + total[:, RANK:]).astype(BF)
    for t in range(NZ):
        zs[t] = jnp.concatenate([part[32 * t:32 * t + 16], part[32 * t + 16:32 * t + 32]], axis=1)
    zr[z] = zs[z]
    reduce.start()
    ring_step(5)
    for j in range(4):
        for way in range(2):
            sheet(way, 1, j).recv()
    quarter = iota((MAIN, 1), 0) % 16 // 4
    zero = jnp.zeros((), BF)

    def project(offsets):
        for o in offsets:
            tell(o).recv()
        blocks = [lax.rem(z + o, NZ) for o in offsets]
        count = 16 * len(blocks)
        main = jnp.zeros((count, TOK), F32)
        rest = jnp.zeros((count, TOK), F32)
        for h in range(2):
            for q in range(4):
                at = QUART * q
                toks = buf[:, :, HALF * h + at:HALF * h + at + QUART].reshape(TOK, QUART)
                tail = jnp.concatenate([wg[h, b, :, HALF:] for b in blocks], axis=0)
                left = jnp.concatenate([wg[h, b, :, at:at + QUART] for b in blocks]
                                       + [jnp.where(quarter[:count] == q, tail, zero)], axis=0)
                both = dot_nt(left, toks)
                main += both[:count]
                rest += both[count:]
        for n, b in enumerate(blocks):
            s = rest[16 * n:16 * n + 8] + rest[16 * n + 8:16 * n + 16]
            s = s[:4] + s[4:]
            tail = jnp.concatenate([s[:, 128 * j:128 * j + 128] for j in range(4)], axis=0)
            rsnd[b] = jnp.concatenate([main[16 * n:16 * n + 16], tail], axis=1).astype(BF)
        for o in offsets:
            if o:
                results.one(o)

    project((1,15,2,14,3,13,4,12,0,))
    ring_step(6)
    project((5,11,))
    reduce.recv()
    red[z] = jnp.sum(zr[...].astype(F32), axis=0).astype(BF)
    share.start()
    ring_step(7)
    project((6,10,))
    ring_end()
    project((7,9,8,))
    share.recv()
    for t in range(NZ):
        sh[32 * t:32 * t + 16] = red[t, :, :RANK]
        sh[32 * t + 16:32 * t + 32] = red[t, :, RANK:]
    wide = jnp.concatenate([sh[...]] * ADP, axis=1)
    expand = dot(jnp.where(ident == group, wide, zero), bv[...].reshape(HOT, COLS))
    expand += dot(jnp.where(ident == group + ADP, wide, zero), hot_b)
    er[...] = expand.astype(BF).reshape(ND, SLOT, COLS)
    back[d] = er[d]
    give_back.start()
    opened.append(results)
    rrcv[z] = rsnd[z]
    results.recv()
    pieces = []
    for g in range(4):
        four = jnp.concatenate([rrcv[4 * g + i] for i in range(4)], axis=1)
        for j in range(5):
            pieces.append(jnp.concatenate(
                [four[:, 640 * i + 128 * j:640 * i + 128 * j + 128] for i in range(4)], axis=1))
    stacked = jnp.concatenate(pieces, axis=0)
    lane_in, lane_out = iota((TOK, TOK), 0), iota((TOK, TOK), 1)
    moved = (lane_in // 32 % 4) * 128 + lane_in // 128 * 32 + lane_in % 32
    turned = dot(stacked, onehot(moved == lane_out))
    for j in range(NC):
        t, k = j // 4, 128 * (j % 4)
        for g in range(4):
            psnd[j, 16 * g:16 * g + 16] = turned[80 * g + 16 * t:80 * g + 16 * t + 16, k:k + 128].astype(BF)
        psnd[j, 64:] = jnp.concatenate(
            [turned[80 * g + 64 + 4 * t:80 * g + 68 + 4 * t, k:k + 128] for g in range(4)], axis=0).astype(BF)
    pout[chip] = psnd[chip]
    plane.start()
    give_back.recv()
    extra = dot_t(back[...].reshape(TOK, COLS), pick[...])
    plane.recv()
    upright = [jnp.concatenate([pout[p, 16 * g:16 * g + 16] for g in range(4)], axis=1).astype(F32) for p in range(NC)]
    for p in range(NC):
        low = pout[p, 64:].astype(F32)
        upright.append(jnp.concatenate([low[4 * g:4 * g + 4] for g in range(4)], axis=1))
    base = jnp.concatenate(upright, axis=0)
    out[...] = (res[...].astype(F32) + base + 0.5 * extra).astype(BF)
    finish()


def local(attention, residual, output_weight, adapter_down_weight, adapter_up_weight, tenant, adapter_slot_index):
    vmem = pl.BlockSpec(memory_space=pltpu.VMEM)
    hbm = pl.BlockSpec(memory_space=pl.ANY)
    dma = pltpu.SemaphoreType.DMA

    def held(*shape, dtype=BF):
        return pltpu.VMEM(shape, dtype)

    return pl.pallas_call(
        kernel,
        out_shape=jax.ShapeDtypeStruct((COLS, TOK), BF),
        in_specs=[vmem, hbm, hbm, hbm, hbm, vmem, vmem],
        out_specs=vmem,
        scratch_shapes=[
            held(REST, HALF), held(COLS, TOK), held(ADP, RANK, COLS), held(ADP, RANK, COLS),
            held(2, NC, 32, COLS), held(NC, 32, COLS), held(NC, 32, COLS), held(NC, 32, COLS), held(2, NC, 32, COLS),
            held(NZ, OWN, COLS), held(NZ, OWN, COLS), held(TOK, TOK),
            held(ND, SLOT, COLS + 64), held(ND, SLOT, COLS + 64),
            held(NZ, 16, 128), held(NZ, 16, 128), held(NZ, 16, 128), held(TOK, RANK),
            held(ND, SLOT, COLS), held(ND, SLOT, COLS),
            held(NC, OWN, WIDTH), held(2, NZ, 16, LANES), held(NZ, 16, 640), held(NZ, 16, 640),
            held(NC, 80, 128), held(NC, 80, 128),
            dma((5,)), dma((2, 11)), dma((3, 2, 4)), dma((3, 2, 4)), dma((2, 8, 2)), dma((2, 8, 2)), dma((NZ,)), dma((NZ,)),
        ],
        compiler_params=pltpu.CompilerParams(collective_id=0, has_side_effects=True, vmem_limit_bytes=56 * 2**20),
    )(attention, residual.T, output_weight.T, adapter_down_weight.transpose(0, 2, 1), adapter_up_weight,
      tenant.reshape(1, REQ), adapter_slot_index.reshape(1, 2 * REQ)).T


def solution(mesh):
    in_specs = (
        P(("dp", "tensor"), None),
        P("dp", "tensor"),
        P(None, "tensor"),
        P("dp", "tensor", None),
        P("dp", None, "tensor"),
        P("dp"),
        P(),
    )
    return jax.shard_map(local, mesh=mesh, in_specs=in_specs, out_specs=P("dp", "tensor"), check_vma=False)
```

time: 115 us -> 101 us (0.88)
  local copies, waits for them, and re-layouts: 11.7 us -> 1.72 us
  Pallas kernels: 103 us -> 99.4 us
    unnamed x3 -> x1, local copies, waits for them, and re-layouts: 9.83 us -> 1.72 us
    pallas_call x1, Pallas kernels: 103 us -> 99.4 us  [local(): pl.pallas_call(kernel, out_shape=jax.ShapeDtypeStruct((COLS, TOK), BF), i...]
    pallas_call x1 -> x0, local copies, waits for them, and re-layouts: 1.88 us -> none  [local(): pl.pallas_call(kernel, out_shape=jax.ShapeDtypeStruct((TOK, COLS), BF), i...]
where the time goes in v2:
time: 101 us
  Pallas kernels  99.4 us (98%)
  local copies, waits for them, and re-layouts  1.72 us (2%)
    pallas_call x1, Pallas kernels, local(): pl.pallas_call(kernel, out_shape=jax.ShapeDtypeStruct((COLS, TOK), BF), i...  99.4 us

profile of v2, /device:TPU:1, one launch (start us, length us, event | category | flops | bytes accessed | tf_op | source)
XLA Modules:
  0.0 101.1 jit_solution(6271176073307325429)
XLA Ops:
  0.0 99.4 %shard_map.73 = bf16[320,512]{1,0:T(8,128)(2,1)} custom-call(bf16[32,5120]{1,0:T(8,128)(2,1)} %att.1, bf16[320,512]{1,0:T(8,128)(2,1)} %bitcast.9, bf16[320,5120]{1,0:T(8,128)(2,1)} %bitcast.6, bf16[8,64,320]{2,1,0:T(8,128)(2,1)} %bitcast.8, bf16[8,64,320]{2,1,0:T(8,128)(2,1)} %b_h.1, s32[1,128]{1,0:T(1,128)} %bitcast.11, s32[1,256]{1,0:T(1,128)} %bitcast.10), custom_call_target="tpu_custom_call" | custom-call | tf_op jit(solution)/shard_map/pallas_call | solution.py:440
  99.4 1.7 %copy.9 = bf16[512,320]{0,1:T(8,128)(2,1)} copy(bf16[512,320]{0,1:T(8,128)(2,1)} %bitcast.7) | data formatting | bytes 655360

commit v3 on v2

--- a/solution.py
+++ b/solution.py
@@ -307,27 +307,29 @@
     half[...] = mine[core] + twin_in[...]
     hot_in[chip] = half[chip]
     scatter.start()
+    ring_step(0)
     line_on()
     sheet_on(0)
     line_end()
-    scatter.recv()
-    hot[core, chip] = jnp.sum(hot_in[...].astype(F32), axis=0).astype(BF)
-    gather.start()
-    ring_step(0)
-    sheet_on(1)
     ring_step(1)
-    sheet_on(2)
-    ring_step(2)
     slices.recv()
     ext = jnp.concatenate([own[...].reshape(TOK, COLS), ids], axis=1)
     pk[...] = dot(pick[...], ext).astype(BF).reshape(ND, SLOT, COLS + 64)
     prcv[d] = pk[d]
     deliver.start()
+    scatter.recv()
+    hot[core, chip] = jnp.sum(hot_in[...].astype(F32), axis=0).astype(BF)
+    gather.start()
+    sheet_on(1)
+    ring_step(2)
+    sheet_on(2)
     ring_step(3)
+    ring_step(4)
     sheet_on(3)
-    ring_step(4)
+    ring_step(5)
     gather.recv()
     swap_hot.start()
+    ring_step(6)
     deliver.recv()
     swap_hot.recv()
     got = prcv[...].reshape(TOK, COLS + 64)
@@ -343,7 +345,7 @@
         zs[t] = jnp.concatenate([part[32 * t:32 * t + 16], part[32 * t + 16:32 * t + 32]], axis=1)
     zr[z] = zs[z]
     reduce.start()
-    ring_step(5)
+    ring_step(7)
     for j in range(4):
         for way in range(2):
             sheet(way, 1, j).recv()
@@ -377,15 +379,11 @@
                 results.one(o)
 
     project((1,15,2,14,3,13,4,12,0,))
-    ring_step(6)
-    project((5,11,))
+    ring_end()
     reduce.recv()
     red[z] = jnp.sum(zr[...].astype(F32), axis=0).astype(BF)
     share.start()
-    ring_step(7)
-    project((6,10,))
-    ring_end()
-    project((7,9,8,))
+    project((5,11,6,10,7,9,8,))
     share.recv()
     for t in range(NZ):
         sh[32 * t:32 * t + 16] = red[t, :, :RANK]

time: 101 us -> 95.4 us (0.945)
  Pallas kernels: 99.4 us -> 93.5 us
    pallas_call x1, Pallas kernels: 99.4 us -> 93.5 us  [local(): pl.pallas_call(kernel, out_shape=jax.ShapeDtypeStruct((COLS, TOK), BF), i...]
where the time goes in v3:
time: 95.4 us; the launch traced here: 95.2 us
  Pallas kernels  93.5 us (98%)
  local copies, waits for them, and re-layouts  1.72 us (2%)
    pallas_call x1, Pallas kernels, local(): pl.pallas_call(kernel, out_shape=jax.ShapeDtypeStruct((COLS, TOK), BF), i...  93.5 us

profile of v3, /device:TPU:1, one launch (start us, length us, event | category | flops | bytes accessed | tf_op | source)
XLA Modules:
  0.0 95.2 jit_solution(18436593131331977730)
XLA Ops:
  0.0 93.5 %shard_map.73 = bf16[320,512]{1,0:T(8,128)(2,1)} custom-call(bf16[32,5120]{1,0:T(8,128)(2,1)} %att.1, bf16[320,512]{1,0:T(8,128)(2,1)} %bitcast.9, bf16[320,5120]{1,0:T(8,128)(2,1)} %bitcast.6, bf16[8,64,320]{2,1,0:T(8,128)(2,1)} %bitcast.8, bf16[8,64,320]{2,1,0:T(8,128)(2,1)} %b_h.1, s32[1,128]{1,0:T(1,128)} %bitcast.11, s32[1,256]{1,0:T(1,128)} %bitcast.10), custom_call_target="tpu_custom_call" | custom-call | tf_op jit(solution)/shard_map/pallas_call | solution.py:438
  93.5 1.7 %copy.9 = bf16[512,320]{0,1:T(8,128)(2,1)} copy(bf16[512,320]{0,1:T(8,128)(2,1)} %bitcast.7) | data formatting | bytes 655360
